TPU v7x, 32 devices: a whole 2x2x4 slice. The times are simulated.
32 devices in a mesh: parts: 2 (over y), grid: 4 (over z), dom: 4 (over x, core).
Axes of the slice: x: 2, y: 2, z: 4, core: 2. Of those that a mesh axis runs over, the one named last changes fastest.
Arguments:
- initial: float32 [8, 512, 4, 128], P(('parts', 'grid'), None, 'dom'), parts along dimension 0, may hold values from -6 to 6
- levels: int32 [8, 2], P(('parts', 'grid')), parts along dimension 0, may hold values from 1 to 7
- coefficients: int32 [8], P(('parts', 'grid')), parts along dimension 0, may hold values from -1 to 1, as said below
- velocity: float32 [8], P('parts'), parts along dimension 0, may hold values from -0.15 to 0.15
- position: int32 [1792], replicated, may hold values from 0 to 1791, each once
Outputs:
- combined: float32 [3584, 4, 128], P(('parts', 'grid'), 'dom'), parts along dimension 0
- result: float32 [8, 512, 4, 128], P(('parts', 'grid'), None, 'dom'), parts along dimension 0
There are 2 independent parts, one for each index of `parts`. A program takes and returns all parts, laid end to end along the dimension named above; an argument that names none is the same for every part. Nothing has to cross between parts.
Inputs may be any that keep to these rules, and one draw needn't show every extreme that they name: `coefficients`: +1 for grids with l1 + l2 = 9, -1 for l1 + l2 = 8.
All inputs are finite; a program needn't handle non-finite values.
Results may differ from a plain program's by a relative error of at most 0.0003.
Values sent between devices are 32-bit elements; how exact they have to be, the bound alone decides.
A program may use at most 64 MiB of HBM per device.

v0:
```python
import functools
from math import comb

import jax
import jax.numpy as jnp
from jax import lax
from jax.experimental import pallas as pl
from jax.experimental.pallas import tpu as pltpu
from jax.sharding import PartitionSpec as P

M = 9
LMIN = 2
STEPS = 4
DIFFUSE = 0.05
TOP = M - LMIN
UNIT = 1 << TOP
PIECES = 4
BLOCK = 64
MESH = pl.DeviceIdType.MESH
F32 = jnp.float32
BF16 = jnp.bfloat16


def coords(flat, level_one, level_two):
    one = jnp.left_shift(jnp.right_shift(flat, level_two), TOP - level_one)
    two = jnp.left_shift(flat & (jnp.left_shift(jnp.int32(1), level_two) - 1), TOP - level_two)
    return one, two


def trailing(coord):
    zeros = jnp.zeros_like(coord)
    for bit in range(1, TOP):
        zeros = zeros + jnp.where((coord & ((1 << bit) - 1)) == 0, 1, 0)
    return zeros


def inverse_width(coord, zeros):
    width = jnp.zeros(coord.shape, F32)
    for bit in range(TOP):
        width = jnp.where(zeros == bit, 0.5**bit, width)
    return jnp.where(coord == 0, 0.0, width)


def hier(coord, zeros):
    index = jnp.right_shift(jnp.full_like(coord, UNIT // 2), zeros)
    return jnp.where(coord == 0, 0, index + jnp.right_shift(coord, zeros + 1))


def sparse_ids(one, two, zeros_one, zeros_two):
    h_one, h_two = hier(one, zeros_one), hier(two, zeros_two)
    bits = jnp.where(one == 0, 0, TOP - zeros_one)
    head = jnp.left_shift(jnp.ones_like(one), jnp.maximum(bits - 1, 0))
    low = h_one * (1 << TOP)
    high = (1 << M) + (bits - 1 - LMIN) * (1 << (M - 1)) + (h_one - head) * jnp.left_shift(
        jnp.ones_like(one), M - bits
    )
    return jnp.where(bits <= LMIN, low, high) + h_two


def split(values):
    high = values.astype(BF16)
    low = (values - high.astype(F32)).astype(BF16)
    return jnp.concatenate([high, low], axis=1)


def product(matrix, values):
    width = values.shape[1]
    both = jnp.dot(matrix, split(values), preferred_element_type=F32)
    return both[:, :width] + both[:, width:]


def kernel(
    doms, grids, lev, coef, vel, pos, start, own_ref, result_ref,
    layers, fields, meta, basis, surplus_of, mats, total,
    layer_send, layer_recv, pass_send, meta_send, meta_recv, right_send, left_send, sur_recv,
):
    rows, lanes = start.shape
    owned = own_ref.shape[0]
    chips = doms // 2
    here = lax.axis_index("dom")
    z = lax.axis_index("grid")
    chip, core = here // 2, lax.rem(here, 2)
    sibling = here + 1 - 2 * core
    level_one, level_two = lev[0, 0], lev[0, 1]
    stride, live = jnp.int32(1), jnp.int32(rows)
    for level in range(1, TOP + 1):
        stride = jnp.where(level_two == level, 1 << level, stride)
    for level in range(M):
        live = jnp.where(level_one + level_two == level, 1 << level, live)

    others = [lax.rem(chip + j, chips) * 2 + core for j in range(1, chips)]
    sources = [lax.rem(chip + chips - j, chips) * 2 + core for j in range(1, chips)]
    peers = [lax.rem(z + j, grids) for j in range(1, grids)]

    barrier = pltpu.get_barrier_semaphore()
    for peer in [sibling] + others:
        pl.semaphore_signal(barrier, inc=1, device_id={"dom": peer}, device_id_type=MESH)
    for peer in peers:
        pl.semaphore_signal(barrier, inc=1, device_id={"grid": peer}, device_id_type=MESH)
    pl.semaphore_wait(barrier, chips + grids - 1)

    piece_rows = rows // PIECES

    def layer_copy(source, slot, piece, target, send):
        at = pl.ds(piece * piece_rows, piece_rows)
        return pltpu.make_async_remote_copy(
            src_ref=source.at[at],
            dst_ref=layers.at[slot, at],
            send_sem=send,
            recv_sem=layer_recv.at[slot, piece],
            device_id={"dom": target},
            device_id_type=MESH,
        )

    for piece in range(PIECES):
        for j, peer in enumerate(others):
            layer_copy(start, here, piece, peer, layer_send.at[j, piece]).start()
    for piece in range(PIECES):
        layer_copy(start, here, piece, sibling, layer_send.at[chips - 1, piece]).start()

    flat = lax.broadcasted_iota(jnp.int32, (1, rows), 1)
    one, two = coords(flat, level_one, level_two)
    zeros_one, zeros_two = trailing(one), trailing(two)
    ids = jnp.where(flat < live, sparse_ids(one, two, zeros_one, zeros_two), -1)
    lines = [
        one.astype(F32), two.astype(F32),
        inverse_width(one, zeros_one), inverse_width(two, zeros_two),
        ids.astype(F32),
    ]
    for line, value in enumerate(lines):
        meta[z, line : line + 1, :] = value
    meta[z, len(lines) :, :] = jnp.zeros((8 - len(lines), rows), F32)

    def meta_copy(j):
        return pltpu.make_async_remote_copy(
            src_ref=meta.at[z],
            dst_ref=meta.at[z],
            send_sem=meta_send.at[j],
            recv_sem=meta_recv.at[z],
            device_id={"grid": peers[j]},
            device_id_type=MESH,
        )

    for j in range(grids - 1):
        meta_copy(j).start()

    def pass_on(piece):
        for j, slot in enumerate(sources):
            layer_copy(start, slot, piece, sibling, layer_send.at[0, 0]).wait_recv()
            layer_copy(layers.at[slot], slot, piece, sibling, pass_send.at[j, piece]).start()

    def column(begin, count):
        return begin + lax.broadcasted_iota(jnp.int32, (count, 1), 0)

    def build_basis(step, carry):
        begin = pl.multiple_of(step * BLOCK, BLOCK)
        row_one, row_two = coords(column(begin, BLOCK), level_one, level_two)

        def factor(row, col):
            width = jnp.where(row == 0, 2 * UNIT - 1, row & (-row))
            apart = (col - row) & (UNIT - 1)
            near = jnp.where(apart == 0, 1.0, jnp.where(apart == width, -0.5, 0.0))
            return near + jnp.where(apart == UNIT - width, -0.5, 0.0)

        basis[pl.ds(begin, BLOCK), :] = (factor(row_one, one) * factor(row_two, two)).astype(BF16)
        return carry

    lax.fori_loop(0, rows // BLOCK, build_basis, 0)
    pass_on(0)

    target = z * owned + lax.broadcasted_iota(jnp.int32, (owned, lanes), 0)
    found = jnp.zeros((owned, lanes), F32)
    for j in range(pos.shape[0]):
        number = lax.broadcasted_iota(jnp.int32, (1, lanes), 1) + j * lanes
        found = found + jnp.where(pos[j : j + 1, :] == target, number.astype(F32), 0.0)
    own_ids = jnp.sum(found, axis=1, keepdims=True)
    pad = mats.shape[1] - rows - owned
    if pad:
        own_ids = jnp.concatenate([own_ids, jnp.full((pad, 1), -2.0, F32)], axis=0)
    pass_on(1)

    def build_mats(g, carry):
        @pl.when(g != z)
        def _():
            pltpu.make_async_remote_copy(
                src_ref=meta.at[g], dst_ref=meta.at[g], send_sem=meta_send.at[0],
                recv_sem=meta_recv.at[g], device_id={"grid": peers[0]}, device_id_type=MESH,
            ).wait_recv()

        mats[g, rows:, :] = jnp.where(own_ids == meta[g, 4:5, :], 1.0, 0.0).astype(BF16)

        def build(step, inner):
            begin = pl.multiple_of(step * BLOCK, BLOCK)
            row_one, row_two = coords(column(begin, BLOCK), level_one, level_two)
            hat = jnp.maximum(
                1.0 - jnp.abs(row_one.astype(F32) - meta[g, 0:1, :]) * meta[g, 2:3, :], 0.0
            ) * jnp.maximum(
                1.0 - jnp.abs(row_two.astype(F32) - meta[g, 1:2, :]) * meta[g, 3:4, :], 0.0
            )
            mats[g, pl.ds(begin, BLOCK), :] = hat.astype(BF16)
            return inner

        return lax.fori_loop(0, rows // BLOCK, build, carry)

    half = grids // 2
    lax.fori_loop(0, half, build_mats, 0)
    pass_on(2)
    lax.fori_loop(half, grids, build_mats, 0)
    pass_on(3)

    ahead, behind = [], []
    for d in range(4):
        speed = vel[d]
        ahead.append(DIFFUSE - jnp.minimum(speed, 0.0))
        behind.append(DIFFUSE + jnp.maximum(speed, 0.0))
    keep = 1.0
    for d in range(4):
        keep = keep - (ahead[d] + behind[d])

    def power(base, count):
        value = 1.0
        for _ in range(count):
            value = value * base
        return value

    weights = []
    for order in range(1, STEPS + 1):
        table = {}
        for i in range(order + 1):
            weight = (
                float(comb(STEPS, order) * comb(order, i))
                * power(ahead[2], i)
                * power(behind[2], order - i)
            )
            offset = (2 * i - order) % doms
            table[offset] = table[offset] + weight if offset in table else weight
        weights.append(table)

    def store_field(which, begin, value):
        fields[which, pl.ds(UNIT + begin, BLOCK), :] = value

    def wrap(which):
        fields[which, 0:UNIT, :] = fields[which, rows : rows + UNIT, :]
        fields[which, rows + UNIT :, :] = fields[which, UNIT : 2 * UNIT, :]

    def periodic(layer, begin):
        first = pl.multiple_of(lax.rem(begin, rows // 2), BLOCK)
        return jnp.where(
            live == rows, layer[pl.ds(begin, BLOCK), :], layer[pl.ds(first, BLOCK), :]
        )

    def load_start(step, carry):
        begin = pl.multiple_of(step * BLOCK, BLOCK)
        store_field(0, begin, periodic(start, begin))
        return carry

    lax.fori_loop(0, rows // BLOCK, load_start, 0)
    wrap(0)

    for piece in range(PIECES):
        layer_copy(start, sibling, piece, sibling, layer_send.at[0, 0]).wait_recv()
        for slot in sources:
            across = slot + 1 - 2 * core
            layer_copy(start, across, piece, sibling, layer_send.at[0, 0]).wait_recv()

    for order in range(1, STEPS + 1):
        now, later = (order + 1) % 2, order % 2
        table = weights[order - 1]

        def advance(step, carry, now=now, later=later, table=table):
            begin = pl.multiple_of(step * BLOCK, BLOCK)
            at = begin + UNIT
            read = lambda shift: fields[now, pl.ds(at + shift, BLOCK), :]
            centre = read(0)
            along = column(begin, BLOCK) & (stride - 1)
            after = jnp.where(along == stride - 1, read(1 - stride), read(1))
            before = jnp.where(along == 0, read(stride - 1), read(-1))
            value = keep * centre
            value = value + ahead[0] * read(stride) + behind[0] * read(-stride)
            value = value + ahead[1] * after + behind[1] * before
            value = value + ahead[3] * pltpu.roll(centre, lanes - 1, 1)
            value = value + behind[3] * pltpu.roll(centre, 1, 1)
            for offset, weight in table.items():
                source = start if offset == 0 else layers.at[lax.rem(here + offset, doms)]
                value = value + weight * periodic(source, begin)
            store_field(later, begin, value)
            return carry

        lax.fori_loop(0, rows // BLOCK, advance, 0)
        if order < STEPS:
            wrap(later)

    inside = lax.broadcasted_iota(jnp.int32, (rows, 1), 0) < live
    values = jnp.where(inside, fields[STEPS % 2, UNIT : UNIT + rows, :], 0.0)
    weight = coef[0].astype(F32)
    surplus = jnp.where(inside, weight * product(basis[...], values), 0.0)
    surplus_of[z] = surplus

    def surplus_copy(slot, target, send):
        return pltpu.make_async_remote_copy(
            src_ref=surplus_of.at[slot],
            dst_ref=surplus_of.at[slot],
            send_sem=send.at[slot],
            recv_sem=sur_recv.at[slot],
            device_id={"grid": target},
            device_id_type=MESH,
        )

    right, left = jnp.minimum(z + 1, grids - 1), jnp.maximum(z - 1, 0)

    @pl.when(z < grids - 1)
    def _():
        surplus_copy(z, right, right_send).start()

    @pl.when(z > 0)
    def _():
        surplus_copy(z, left, left_send).start()

    total[...] = product(mats[z], surplus)

    def exchange(step, carry):
        low, high = z - step, z + step

        @pl.when(low >= 0)
        def _():
            surplus_copy(low, left, left_send).wait_recv()

            @pl.when(z < grids - 1)
            def _():
                surplus_copy(low, right, right_send).start()

        @pl.when(high < grids)
        def _():
            surplus_copy(high, right, right_send).wait_recv()

            @pl.when(z > 0)
            def _():
                surplus_copy(high, left, left_send).start()

        @pl.when(low >= 0)
        def _():
            total[...] += product(mats[low], surplus_of[low])

        @pl.when(high < grids)
        def _():
            total[...] += product(mats[high], surplus_of[high])

        return carry

    lax.fori_loop(1, grids, exchange, 0)

    own_ref[...] = total[rows : rows + owned, :]
    result_ref[...] = jnp.where(inside, total[0:rows, :], 0.0)

    for piece in range(PIECES):
        for j, peer in enumerate(others):
            layer_copy(start, here, piece, peer, layer_send.at[j, piece]).wait_send()
            layer_copy(start, here, piece, peer, pass_send.at[j, piece]).wait_send()
        layer_copy(start, here, piece, sibling, layer_send.at[chips - 1, piece]).wait_send()
    for j in range(grids - 1):
        meta_copy(j).wait_send()

    def drain(slot, carry):
        @pl.when((z < grids - 1) & (slot <= z))
        def _():
            surplus_copy(slot, right, right_send).wait_send()

        @pl.when((z > 0) & (slot >= z))
        def _():
            surplus_copy(slot, left, left_send).wait_send()

        return carry

    lax.fori_loop(0, grids, drain, 0)


def local(doms, grids, initial, levels, coefficients, velocity, position):
    rows, lanes = initial.shape[1], initial.shape[3]
    owned = position.shape[0] // grids
    padded = -(-owned // 16) * 16
    chips = doms // 2
    vmem = pl.BlockSpec(memory_space=pltpu.VMEM)
    smem = pl.BlockSpec(memory_space=pltpu.SMEM)
    sems = pltpu.SemaphoreType.DMA
    own, result = pl.pallas_call(
        functools.partial(kernel, doms, grids),
        out_shape=[
            jax.ShapeDtypeStruct((owned, lanes), F32),
            jax.ShapeDtypeStruct((rows, lanes), F32),
        ],
        in_specs=[smem, smem, smem, vmem, vmem],
        out_specs=[vmem, vmem],
        scratch_shapes=[
            pltpu.VMEM((doms, rows, lanes), F32),
            pltpu.VMEM((2, rows + 2 * UNIT, lanes), F32),
            pltpu.VMEM((grids, 8, rows), F32),
            pltpu.VMEM((rows, rows), BF16),
            pltpu.VMEM((grids, rows, lanes), F32),
            pltpu.VMEM((grids, rows + padded, rows), BF16),
            pltpu.VMEM((rows + padded, lanes), F32),
            sems((chips, PIECES)),
            sems((doms, PIECES)),
            sems((chips, PIECES)),
            sems((grids,)),
            sems((grids,)),
            sems((grids,)),
            sems((grids,)),
            sems((grids,)),
        ],
        compiler_params=pltpu.CompilerParams(
            collective_id=0, has_side_effects=True, vmem_limit_bytes=48 << 20
        ),
    )(
        levels, coefficients, velocity,
        position.reshape(-1, lanes), initial.reshape(rows, lanes),
    )
    return own[:, None, :], result[None, :, None, :]


def solution(mesh):
    return jax.shard_map(
        functools.partial(local, mesh.shape["dom"], mesh.shape["grid"]),
        mesh=mesh,
        in_specs=(
            P(("parts", "grid"), None, "dom", None),
            P(("parts", "grid"), None),
            P(("parts", "grid")),
            P("parts"),
            P(),
        ),
        out_specs=(P(("parts", "grid"), "dom", None), P(("parts", "grid"), None, "dom", None)),
        check_vma=False,
    )
```

profile of v0, /device:TPU:0, one launch (start us, length us, event | category | flops | bytes accessed | tf_op | source)
XLA Modules:
  0.0 45.6 jit_solution(4652539901062353640)
XLA Ops:
  1.3 0.0 copy-start.2
  1.3 0.0 copy-start.3
  1.3 0.6 %copy-done.2 = s32[1,2]{1,0:T(1,128)S(1)} copy-done((s32[1,2]{1,0:T(1,128)S(1)}, s32[1,2]{1,0:T(1,128)}, u32[]{:S(2)}) %copy-start.2) | copy-done | bytes 32
  1.9 0.0 copy-done.3
  1.9 0.0 copy-start
  2.0 0.9 %copy-done = f32[1,512,1,128]{3,2,1,0:T(1,128)S(1)} copy-done((f32[1,512,1,128]{3,2,1,0:T(1,128)S(1)}, f32[1,512,1,128]{3,2,1,0:T(1,128)}, u32[]{:S(2)}) %copy-start) | copy-done | bytes 262168
  2.9 0.0 copy-start.1
  2.9 0.7 %copy-done.1 = s32[1792]{0:T(1024)S(1)} copy-done((s32[1792]{0:T(1024)S(1)}, s32[1792]{0:T(1024)}, u32[]{:S(2)}) %copy-start.1) | copy-done | bytes 7192
  3.6 40.6 %shard_map.68 = (f32[448,128]{1,0:T(8,128)S(1)}, f32[512,128]{1,0:T(8,128)S(1)}) custom-call(s32[1,2]{1,0:T(1,128)S(1)} %copy-done.2, s32[1]{0:T(128)S(6)} %copy.11.coef, f32[4]{0:T(128)S(1)} %copy-done.3, s32[14,128]{1,0:T(8,128)S(1)} %bitcast.11, f32[512,128]{1,0:T(8,128)S(1)} %bitcast.8), custom_call_target="tpu_custom_call" | custom-call | tf_op jit(solution)/shard_map/pallas_call | solution.py:385
  44.2 0.7 %copy.12 = f32[448,1,128]{2,1,0:T(1,128)} copy(f32[448,1,128]{2,1,0:T(1,128)S(1)} %bitcast.10) | data formatting | bytes 458752
  44.9 0.7 %copy.13 = f32[1,512,1,128]{3,2,1,0:T(1,128)} copy(f32[1,512,1,128]{3,2,1,0:T(1,128)S(1)} %bitcast.9) | data formatting | bytes 524288
Async XLA Ops:
  1.3 0.7 %copy-start.2 = (s32[1,2]{1,0:T(1,128)S(1)}, s32[1,2]{1,0:T(1,128)}, u32[]{:S(2)}) copy-start(s32[1,2]{1,0:T(1,128)} %lev.1) | copy-start | bytes 28
  1.3 0.7 %copy-start.3 = (f32[4]{0:T(128)S(1)}, f32[4]{0:T(128)}, u32[]{:S(2)}) copy-start(f32[4]{0:T(128)} %vel.1) | copy-start | bytes 52
  1.9 0.9 %copy-start = (f32[1,512,1,128]{3,2,1,0:T(1,128)S(1)}, f32[1,512,1,128]{3,2,1,0:T(1,128)}, u32[]{:S(2)}) copy-start(f32[1,512,1,128]{3,2,1,0:T(1,128)} %param.5) | copy-start | bytes 786436
  2.9 0.7 %copy-start.1 = (s32[1792]{0:T(1024)S(1)}, s32[1792]{0:T(1024)}, u32[]{:S(2)}) copy-start(s32[1792]{0:T(1024)} %param.9) | copy-start | bytes 21508
where the time goes:
time: 45.8 us; the launch traced here: 45.6 us
  Pallas kernels  40.6 us (89%)
  local copies, waits for them, and re-layouts  3.69 us (8%)
  between operations  1.3 us (3%)
    pallas_call x1, Pallas kernels, local(): pl.pallas_call(functools.partial(kernel, doms, grids), out_shape=[jax.Sha...  40.6 us
    unnamed x10, local copies, waits for them, and re-layouts  3.69 us

commit v1 on v0

--- a/solution.py
+++ b/solution.py
@@ -14,7 +14,8 @@
 DIFFUSE = 0.05
 TOP = M - LMIN
 UNIT = 1 << TOP
-PIECES = 4
+CHUNKS = 4
+HALO = 8
 BLOCK = 64
 MESH = pl.DeviceIdType.MESH
 F32 = jnp.float32
@@ -60,18 +61,20 @@
 def split(values):
     high = values.astype(BF16)
     low = (values - high.astype(F32)).astype(BF16)
-    return jnp.concatenate([high, low], axis=1)
+    return jnp.concatenate([high, low], axis=0)
 
 
 def product(matrix, values):
-    width = values.shape[1]
-    both = jnp.dot(matrix, split(values), preferred_element_type=F32)
+    width = values.shape[0]
+    both = lax.dot_general(
+        matrix, split(values), (((1,), (1,)), ((), ())), preferred_element_type=F32
+    )
     return both[:, :width] + both[:, width:]
 
 
 def kernel(
     doms, grids, lev, coef, vel, pos, start, own_ref, result_ref,
-    layers, fields, meta, basis, surplus_of, mats, total,
+    layers, meta, basis, surplus_of, mats, total,
     layer_send, layer_recv, pass_send, meta_send, meta_recv, right_send, left_send, sur_recv,
 ):
     rows, lanes = start.shape
@@ -99,12 +102,19 @@
         pl.semaphore_signal(barrier, inc=1, device_id={"grid": peer}, device_id_type=MESH)
     pl.semaphore_wait(barrier, chips + grids - 1)
 
-    piece_rows = rows // PIECES
-
-    def layer_copy(source, slot, piece, target, send):
-        at = pl.ds(piece * piece_rows, piece_rows)
+    part = lanes // CHUNKS
+    reach = part + 2 * HALO
+    whole = jnp.transpose(start[...])
+    low_half, high_half = whole[:, : rows // 2], whole[:, rows // 2 :]
+    whole = jnp.concatenate([low_half, jnp.where(live == rows, high_half, low_half)], axis=1)
+    layers[here, HALO : HALO + lanes, :] = whole
+    layers[here, 0:HALO, :] = whole[lanes - HALO :, :]
+    layers[here, HALO + lanes :, :] = whole[0:HALO, :]
+
+    def layer_copy(slot, piece, target, send):
+        at = pl.ds(0, reach) if piece == 0 else pl.ds(piece * part + 2 * HALO, part)
         return pltpu.make_async_remote_copy(
-            src_ref=source.at[at],
+            src_ref=layers.at[slot, at],
             dst_ref=layers.at[slot, at],
             send_sem=send,
             recv_sem=layer_recv.at[slot, piece],
@@ -112,11 +122,11 @@
             device_id_type=MESH,
         )
 
-    for piece in range(PIECES):
+    for piece in range(CHUNKS):
         for j, peer in enumerate(others):
-            layer_copy(start, here, piece, peer, layer_send.at[j, piece]).start()
-    for piece in range(PIECES):
-        layer_copy(start, here, piece, sibling, layer_send.at[chips - 1, piece]).start()
+            layer_copy(here, piece, peer, layer_send.at[j, piece]).start()
+    for piece in range(CHUNKS):
+        layer_copy(here, piece, sibling, layer_send.at[chips - 1, piece]).start()
 
     flat = lax.broadcasted_iota(jnp.int32, (1, rows), 1)
     one, two = coords(flat, level_one, level_two)
@@ -146,8 +156,10 @@
 
     def pass_on(piece):
         for j, slot in enumerate(sources):
-            layer_copy(start, slot, piece, sibling, layer_send.at[0, 0]).wait_recv()
-            layer_copy(layers.at[slot], slot, piece, sibling, pass_send.at[j, piece]).start()
+            layer_copy(slot, piece, sibling, layer_send.at[0, 0]).wait_recv()
+            layer_copy(slot, piece, sibling, pass_send.at[j, piece]).start()
+
+    inside = flat < live
 
     def column(begin, count):
         return begin + lax.broadcasted_iota(jnp.int32, (count, 1), 0)
@@ -157,8 +169,8 @@
         row_one, row_two = coords(column(begin, BLOCK), level_one, level_two)
 
         def factor(row, col):
-            width = jnp.where(row == 0, 2 * UNIT - 1, row & (-row))
-            apart = (col - row) & (UNIT - 1)
+            width = jnp.where(col == 0, 2 * UNIT - 1, col & (-col))
+            apart = (row - col) & (UNIT - 1)
             near = jnp.where(apart == 0, 1.0, jnp.where(apart == width, -0.5, 0.0))
             return near + jnp.where(apart == UNIT - width, -0.5, 0.0)
 
@@ -166,7 +178,6 @@
         return carry
 
     lax.fori_loop(0, rows // BLOCK, build_basis, 0)
-    pass_on(0)
 
     target = z * owned + lax.broadcasted_iota(jnp.int32, (owned, lanes), 0)
     found = jnp.zeros((owned, lanes), F32)
@@ -177,7 +188,6 @@
     pad = mats.shape[1] - rows - owned
     if pad:
         own_ids = jnp.concatenate([own_ids, jnp.full((pad, 1), -2.0, F32)], axis=0)
-    pass_on(1)
 
     def build_mats(g, carry):
         @pl.when(g != z)
@@ -201,12 +211,6 @@
             return inner
 
         return lax.fori_loop(0, rows // BLOCK, build, carry)
-
-    half = grids // 2
-    lax.fori_loop(0, half, build_mats, 0)
-    pass_on(2)
-    lax.fori_loop(half, grids, build_mats, 0)
-    pass_on(3)
 
     ahead, behind = [], []
     for d in range(4):
@@ -236,106 +240,83 @@
             table[offset] = table[offset] + weight if offset in table else weight
         weights.append(table)
 
-    def store_field(which, begin, value):
-        fields[which, pl.ds(UNIT + begin, BLOCK), :] = value
-
-    def wrap(which):
-        fields[which, 0:UNIT, :] = fields[which, rows : rows + UNIT, :]
-        fields[which, rows + UNIT :, :] = fields[which, UNIT : 2 * UNIT, :]
-
-    def periodic(layer, begin):
-        first = pl.multiple_of(lax.rem(begin, rows // 2), BLOCK)
-        return jnp.where(
-            live == rows, layer[pl.ds(begin, BLOCK), :], layer[pl.ds(first, BLOCK), :]
-        )
-
-    def load_start(step, carry):
-        begin = pl.multiple_of(step * BLOCK, BLOCK)
-        store_field(0, begin, periodic(start, begin))
-        return carry
-
-    lax.fori_loop(0, rows // BLOCK, load_start, 0)
-    wrap(0)
-
-    for piece in range(PIECES):
-        layer_copy(start, sibling, piece, sibling, layer_send.at[0, 0]).wait_recv()
-        for slot in sources:
-            across = slot + 1 - 2 * core
-            layer_copy(start, across, piece, sibling, layer_send.at[0, 0]).wait_recv()
-
-    for order in range(1, STEPS + 1):
-        now, later = (order + 1) % 2, order % 2
-        table = weights[order - 1]
-
-        def advance(step, carry, now=now, later=later, table=table):
-            begin = pl.multiple_of(step * BLOCK, BLOCK)
-            at = begin + UNIT
-            read = lambda shift: fields[now, pl.ds(at + shift, BLOCK), :]
-            centre = read(0)
-            along = column(begin, BLOCK) & (stride - 1)
-            after = jnp.where(along == stride - 1, read(1 - stride), read(1))
-            before = jnp.where(along == 0, read(stride - 1), read(-1))
-            value = keep * centre
-            value = value + ahead[0] * read(stride) + behind[0] * read(-stride)
-            value = value + ahead[1] * after + behind[1] * before
-            value = value + ahead[3] * pltpu.roll(centre, lanes - 1, 1)
-            value = value + behind[3] * pltpu.roll(centre, 1, 1)
-            for offset, weight in table.items():
-                source = start if offset == 0 else layers.at[lax.rem(here + offset, doms)]
-                value = value + weight * periodic(source, begin)
-            store_field(later, begin, value)
-            return carry
-
-        lax.fori_loop(0, rows // BLOCK, advance, 0)
-        if order < STEPS:
-            wrap(later)
-
-    inside = lax.broadcasted_iota(jnp.int32, (rows, 1), 0) < live
-    values = jnp.where(inside, fields[STEPS % 2, UNIT : UNIT + rows, :], 0.0)
+    along = flat & (stride - 1)
+    first, last = along == 0, along == stride - 1
     weight = coef[0].astype(F32)
-    surplus = jnp.where(inside, weight * product(basis[...], values), 0.0)
-    surplus_of[z] = surplus
-
-    def surplus_copy(slot, target, send):
+
+    def advance(value):
+        shifted = lambda count: pltpu.roll(value, count, 1)
+        after = jnp.where(last, shifted(stride - 1), shifted(rows - 1))
+        before = jnp.where(first, shifted(rows + 1 - stride), shifted(1))
+        moved = keep * value + ahead[1] * after + behind[1] * before
+        moved = moved + ahead[0] * shifted(rows - stride) + behind[0] * shifted(stride)
+        moved = moved + ahead[3] * pltpu.roll(value, reach - 1, 0)
+        return moved + behind[3] * pltpu.roll(value, 1, 0)
+
+    def surplus_part(chunk):
+        at = pl.ds(chunk * part, reach)
+        value = layers[here, at, :]
+        for table in weights:
+            value = advance(value)
+            for offset, factor in table.items():
+                value = value + factor * layers[lax.rem(here + offset, doms), at, :]
+        value = jnp.where(inside, value[HALO : HALO + part, :], 0.0)
+        both = jnp.dot(split(value), basis[...], preferred_element_type=F32)
+        return jnp.where(inside, weight * (both[:part, :] + both[part:, :]), 0.0)
+
+    def surplus_copy(slot, chunk, target, send):
+        at = pl.ds(chunk * part, part)
         return pltpu.make_async_remote_copy(
-            src_ref=surplus_of.at[slot],
-            dst_ref=surplus_of.at[slot],
-            send_sem=send.at[slot],
-            recv_sem=sur_recv.at[slot],
+            src_ref=surplus_of.at[slot, at],
+            dst_ref=surplus_of.at[slot, at],
+            send_sem=send.at[slot, chunk],
+            recv_sem=sur_recv.at[slot, chunk],
             device_id={"grid": target},
             device_id_type=MESH,
         )
 
     right, left = jnp.minimum(z + 1, grids - 1), jnp.maximum(z - 1, 0)
 
-    @pl.when(z < grids - 1)
-    def _():
-        surplus_copy(z, right, right_send).start()
-
-    @pl.when(z > 0)
-    def _():
-        surplus_copy(z, left, left_send).start()
-
-    total[...] = product(mats[z], surplus)
+    for chunk in range(CHUNKS):
+        pass_on(chunk)
+        layer_copy(sibling, chunk, sibling, layer_send.at[0, 0]).wait_recv()
+        for slot in sources:
+            across = slot + 1 - 2 * core
+            layer_copy(across, chunk, sibling, layer_send.at[0, 0]).wait_recv()
+        surplus_of[z, chunk * part : (chunk + 1) * part, :] = surplus_part(chunk)
+
+        @pl.when(z < grids - 1)
+        def _(chunk=chunk):
+            surplus_copy(z, chunk, right, right_send).start()
+
+        @pl.when(z > 0)
+        def _(chunk=chunk):
+            surplus_copy(z, chunk, left, left_send).start()
+
+        lax.fori_loop(grids * chunk // CHUNKS, grids * (chunk + 1) // CHUNKS, build_mats, 0)
+
+    total[...] = product(mats[z], surplus_of[z])
 
     def exchange(step, carry):
         low, high = z - step, z + step
 
-        @pl.when(low >= 0)
-        def _():
-            surplus_copy(low, left, left_send).wait_recv()
-
-            @pl.when(z < grids - 1)
-            def _():
-                surplus_copy(low, right, right_send).start()
-
-        @pl.when(high < grids)
-        def _():
-            surplus_copy(high, right, right_send).wait_recv()
-
-            @pl.when(z > 0)
-            def _():
-                surplus_copy(high, left, left_send).start()
+        for chunk in range(CHUNKS):
+
+            @pl.when(low >= 0)
+            def _(chunk=chunk):
+                surplus_copy(low, chunk, left, left_send).wait_recv()
+
+                @pl.when(z < grids - 1)
+                def _():
+                    surplus_copy(low, chunk, right, right_send).start()
+
+            @pl.when(high < grids)
+            def _(chunk=chunk):
+                surplus_copy(high, chunk, right, right_send).wait_recv()
+
+                @pl.when(z > 0)
+                def _():
+                    surplus_copy(high, chunk, left, left_send).start()
 
         @pl.when(low >= 0)
         def _():
@@ -350,24 +331,28 @@
     lax.fori_loop(1, grids, exchange, 0)
 
     own_ref[...] = total[rows : rows + owned, :]
-    result_ref[...] = jnp.where(inside, total[0:rows, :], 0.0)
-
-    for piece in range(PIECES):
+    result_ref[...] = jnp.where(
+        lax.broadcasted_iota(jnp.int32, (rows, 1), 0) < live, total[0:rows, :], 0.0
+    )
+
+    for piece in range(CHUNKS):
         for j, peer in enumerate(others):
-            layer_copy(start, here, piece, peer, layer_send.at[j, piece]).wait_send()
-            layer_copy(start, here, piece, peer, pass_send.at[j, piece]).wait_send()
-        layer_copy(start, here, piece, sibling, layer_send.at[chips - 1, piece]).wait_send()
+            layer_copy(here, piece, peer, layer_send.at[j, piece]).wait_send()
+            layer_copy(here, piece, peer, pass_send.at[j, piece]).wait_send()
+        layer_copy(here, piece, sibling, layer_send.at[chips - 1, piece]).wait_send()
     for j in range(grids - 1):
         meta_copy(j).wait_send()
 
     def drain(slot, carry):
-        @pl.when((z < grids - 1) & (slot <= z))
-        def _():
-            surplus_copy(slot, right, right_send).wait_send()
-
-        @pl.when((z > 0) & (slot >= z))
-        def _():
-            surplus_copy(slot, left, left_send).wait_send()
+        for chunk in range(CHUNKS):
+
+            @pl.when((z < grids - 1) & (slot <= z))
+            def _(chunk=chunk):
+                surplus_copy(slot, chunk, right, right_send).wait_send()
+
+            @pl.when((z > 0) & (slot >= z))
+            def _(chunk=chunk):
+                surplus_copy(slot, chunk, left, left_send).wait_send()
 
         return carry
 
@@ -391,21 +376,20 @@
         in_specs=[smem, smem, smem, vmem, vmem],
         out_specs=[vmem, vmem],
         scratch_shapes=[
-            pltpu.VMEM((doms, rows, lanes), F32),
-            pltpu.VMEM((2, rows + 2 * UNIT, lanes), F32),
+            pltpu.VMEM((doms, lanes + 2 * HALO, rows), F32),
             pltpu.VMEM((grids, 8, rows), F32),
             pltpu.VMEM((rows, rows), BF16),
-            pltpu.VMEM((grids, rows, lanes), F32),
+            pltpu.VMEM((grids, lanes, rows), F32),
             pltpu.VMEM((grids, rows + padded, rows), BF16),
             pltpu.VMEM((rows + padded, lanes), F32),
-            sems((chips, PIECES)),
-            sems((doms, PIECES)),
-            sems((chips, PIECES)),
+            sems((chips, CHUNKS)),
+            sems((doms, CHUNKS)),
+            sems((chips, CHUNKS)),
             sems((grids,)),
             sems((grids,)),
-            sems((grids,)),
-            sems((grids,)),
-            sems((grids,)),
+            sems((grids, CHUNKS)),
+            sems((grids, CHUNKS)),
+            sems((grids, CHUNKS)),
         ],
         compiler_params=pltpu.CompilerParams(
             collective_id=0, has_side_effects=True, vmem_limit_bytes=48 << 20

time: 45.8 us -> 40.8 us (0.89)
  Pallas kernels: 40.6 us -> 35.6 us
    pallas_call x1, Pallas kernels: 40.6 us -> 35.6 us  [local(): pl.pallas_call(functools.partial(kernel, doms, grids), out_shape=[jax.Sha...]
where the time goes in v1:
time: 40.8 us; the launch traced here: 40.6 us
  Pallas kernels  35.6 us (87%)
  local copies, waits for them, and re-layouts  3.69 us (9%)
  between operations  1.3 us (3%)
    pallas_call x1, Pallas kernels, local(): pl.pallas_call(functools.partial(kernel, doms, grids), out_shape=[jax.Sha...  35.6 us
    unnamed x10, local copies, waits for them, and re-layouts  3.69 us

profile of v1, /device:TPU:0, one launch (start us, length us, event | category | flops | bytes accessed | tf_op | source)
XLA Modules:
  0.0 40.6 jit_solution(5974673228466393446)
XLA Ops:
  1.3 0.0 copy-start.2
  1.3 0.0 copy-start.3
  1.3 0.6 %copy-done.2 = s32[1,2]{1,0:T(1,128)S(1)} copy-done((s32[1,2]{1,0:T(1,128)S(1)}, s32[1,2]{1,0:T(1,128)}, u32[]{:S(2)}) %copy-start.2) | copy-done | bytes 32
  1.9 0.0 copy-done.3
  1.9 0.0 copy-start
  2.0 0.9 %copy-done = f32[1,512,1,128]{3,2,1,0:T(1,128)S(1)} copy-done((f32[1,512,1,128]{3,2,1,0:T(1,128)S(1)}, f32[1,512,1,128]{3,2,1,0:T(1,128)}, u32[]{:S(2)}) %copy-start) | copy-done | bytes 262168
  2.9 0.0 copy-start.1
  2.9 0.7 %copy-done.1 = s32[1792]{0:T(1024)S(1)} copy-done((s32[1792]{0:T(1024)S(1)}, s32[1792]{0:T(1024)}, u32[]{:S(2)}) %copy-start.1) | copy-done | bytes 7192
  3.6 35.6 %shard_map.68 = (f32[448,128]{1,0:T(8,128)S(1)}, f32[512,128]{1,0:T(8,128)S(1)}) custom-call(s32[1,2]{1,0:T(1,128)S(1)} %copy-done.2, s32[1]{0:T(128)S(6)} %copy.11.coef, f32[4]{0:T(128)S(1)} %copy-done.3, s32[14,128]{1,0:T(8,128)S(1)} %bitcast.11, f32[512,128]{1,0:T(8,128)S(1)} %bitcast.8), custom_call_target="tpu_custom_call" | custom-call | tf_op jit(solution)/shard_map/pallas_call | solution.py:370
  39.2 0.7 %copy.12 = f32[448,1,128]{2,1,0:T(1,128)} copy(f32[448,1,128]{2,1,0:T(1,128)S(1)} %bitcast.10) | data formatting | bytes 458752
  39.9 0.7 %copy.13 = f32[1,512,1,128]{3,2,1,0:T(1,128)} copy(f32[1,512,1,128]{3,2,1,0:T(1,128)S(1)} %bitcast.9) | data formatting | bytes 524288
Async XLA Ops:
  1.3 0.7 %copy-start.2 = (s32[1,2]{1,0:T(1,128)S(1)}, s32[1,2]{1,0:T(1,128)}, u32[]{:S(2)}) copy-start(s32[1,2]{1,0:T(1,128)} %lev.1) | copy-start | bytes 28
  1.3 0.7 %copy-start.3 = (f32[4]{0:T(128)S(1)}, f32[4]{0:T(128)}, u32[]{:S(2)}) copy-start(f32[4]{0:T(128)} %vel.1) | copy-start | bytes 52
  1.9 0.9 %copy-start = (f32[1,512,1,128]{3,2,1,0:T(1,128)S(1)}, f32[1,512,1,128]{3,2,1,0:T(1,128)}, u32[]{:S(2)}) copy-start(f32[1,512,1,128]{3,2,1,0:T(1,128)} %param.5) | copy-start | bytes 786436
  2.9 0.7 %copy-start.1 = (s32[1792]{0:T(1024)S(1)}, s32[1792]{0:T(1024)}, u32[]{:S(2)}) copy-start(s32[1792]{0:T(1024)} %param.9) | copy-start | bytes 21508

commit v2 on v1

--- a/solution.py
+++ b/solution.py
@@ -14,7 +14,10 @@
 DIFFUSE = 0.05
 TOP = M - LMIN
 UNIT = 1 << TOP
-CHUNKS = 4
+SHARES = (4, 4, 4, 4)
+CHUNKS = len(SHARES)
+STARTS = [sum(SHARES[:c]) for c in range(CHUNKS + 1)]
+LAG = 2
 HALO = 8
 BLOCK = 64
 MESH = pl.DeviceIdType.MESH
@@ -73,10 +76,14 @@
 
 
 def kernel(
-    doms, grids, lev, coef, vel, pos, start, own_ref, result_ref,
-    layers, meta, basis, surplus_of, mats, total,
-    layer_send, layer_recv, pass_send, meta_send, meta_recv, right_send, left_send, sur_recv,
+    doms, grids, lev, coef, vel, pos_ref, start_ref, own_ref, result_ref,
+    pos, start, layers, meta, basis, surplus_of, mats, total,
+    load_sem, layer_send, layer_recv, pass_send, meta_right, meta_left, meta_recv, right_send, left_send, sur_recv,
 ):
+    load_start = pltpu.make_async_copy(start_ref, start, load_sem.at[0])
+    load_pos = pltpu.make_async_copy(pos_ref, pos, load_sem.at[1])
+    load_start.start()
+    load_pos.start()
     rows, lanes = start.shape
     owned = own_ref.shape[0]
     chips = doms // 2
@@ -93,17 +100,23 @@
 
     others = [lax.rem(chip + j, chips) * 2 + core for j in range(1, chips)]
     sources = [lax.rem(chip + chips - j, chips) * 2 + core for j in range(1, chips)]
-    peers = [lax.rem(z + j, grids) for j in range(1, grids)]
+    right, left = jnp.minimum(z + 1, grids - 1), jnp.maximum(z - 1, 0)
+    has_right, has_left = z < grids - 1, z > 0
 
     barrier = pltpu.get_barrier_semaphore()
     for peer in [sibling] + others:
         pl.semaphore_signal(barrier, inc=1, device_id={"dom": peer}, device_id_type=MESH)
-    for peer in peers:
-        pl.semaphore_signal(barrier, inc=1, device_id={"grid": peer}, device_id_type=MESH)
-    pl.semaphore_wait(barrier, chips + grids - 1)
-
-    part = lanes // CHUNKS
-    reach = part + 2 * HALO
+
+    @pl.when(has_right)
+    def _():
+        pl.semaphore_signal(barrier, inc=1, device_id={"grid": right}, device_id_type=MESH)
+
+    @pl.when(has_left)
+    def _():
+        pl.semaphore_signal(barrier, inc=1, device_id={"grid": left}, device_id_type=MESH)
+
+    unit = lanes // STARTS[-1]
+    load_start.wait()
     whole = jnp.transpose(start[...])
     low_half, high_half = whole[:, : rows // 2], whole[:, rows // 2 :]
     whole = jnp.concatenate([low_half, jnp.where(live == rows, high_half, low_half)], axis=1)
@@ -112,7 +125,9 @@
     layers[here, HALO + lanes :, :] = whole[0:HALO, :]
 
     def layer_copy(slot, piece, target, send):
-        at = pl.ds(0, reach) if piece == 0 else pl.ds(piece * part + 2 * HALO, part)
+        begin = 2 * HALO if piece else 0
+        begin, end = begin + STARTS[piece] * unit, 2 * HALO + STARTS[piece + 1] * unit
+        at = pl.ds(begin, end - begin)
         return pltpu.make_async_remote_copy(
             src_ref=layers.at[slot, at],
             dst_ref=layers.at[slot, at],
@@ -121,12 +136,6 @@
             device_id={"dom": target},
             device_id_type=MESH,
         )
-
-    for piece in range(CHUNKS):
-        for j, peer in enumerate(others):
-            layer_copy(here, piece, peer, layer_send.at[j, piece]).start()
-    for piece in range(CHUNKS):
-        layer_copy(here, piece, sibling, layer_send.at[chips - 1, piece]).start()
 
     flat = lax.broadcasted_iota(jnp.int32, (1, rows), 1)
     one, two = coords(flat, level_one, level_two)
@@ -141,18 +150,31 @@
         meta[z, line : line + 1, :] = value
     meta[z, len(lines) :, :] = jnp.zeros((8 - len(lines), rows), F32)
 
-    def meta_copy(j):
+    neighbours = has_right.astype(jnp.int32) + has_left.astype(jnp.int32)
+    pl.semaphore_wait(barrier, chips + neighbours)
+    for piece in range(CHUNKS):
+        for j, peer in enumerate(others):
+            layer_copy(here, piece, peer, layer_send.at[j, piece]).start()
+    for piece in range(CHUNKS):
+        layer_copy(here, piece, sibling, layer_send.at[chips - 1, piece]).start()
+
+    def meta_copy(slot, target, send):
         return pltpu.make_async_remote_copy(
-            src_ref=meta.at[z],
-            dst_ref=meta.at[z],
-            send_sem=meta_send.at[j],
-            recv_sem=meta_recv.at[z],
-            device_id={"grid": peers[j]},
+            src_ref=meta.at[slot],
+            dst_ref=meta.at[slot],
+            send_sem=send.at[slot],
+            recv_sem=meta_recv.at[slot],
+            device_id={"grid": target},
             device_id_type=MESH,
         )
 
-    for j in range(grids - 1):
-        meta_copy(j).start()
+    @pl.when(has_right)
+    def _():
+        meta_copy(z, right, meta_right).start()
+
+    @pl.when(has_left)
+    def _():
+        meta_copy(z, left, meta_left).start()
 
     def pass_on(piece):
         for j, slot in enumerate(sources):
@@ -180,6 +202,7 @@
     lax.fori_loop(0, rows // BLOCK, build_basis, 0)
 
     target = z * owned + lax.broadcasted_iota(jnp.int32, (owned, lanes), 0)
+    load_pos.wait()
     found = jnp.zeros((owned, lanes), F32)
     for j in range(pos.shape[0]):
         number = lax.broadcasted_iota(jnp.int32, (1, lanes), 1) + j * lanes
@@ -189,14 +212,7 @@
     if pad:
         own_ids = jnp.concatenate([own_ids, jnp.full((pad, 1), -2.0, F32)], axis=0)
 
-    def build_mats(g, carry):
-        @pl.when(g != z)
-        def _():
-            pltpu.make_async_remote_copy(
-                src_ref=meta.at[g], dst_ref=meta.at[g], send_sem=meta_send.at[0],
-                recv_sem=meta_recv.at[g], device_id={"grid": peers[0]}, device_id_type=MESH,
-            ).wait_recv()
-
+    def build_mats(g):
         mats[g, rows:, :] = jnp.where(own_ids == meta[g, 4:5, :], 1.0, 0.0).astype(BF16)
 
         def build(step, inner):
@@ -210,7 +226,37 @@
             mats[g, pl.ds(begin, BLOCK), :] = hat.astype(BF16)
             return inner
 
-        return lax.fori_loop(0, rows // BLOCK, build, carry)
+        lax.fori_loop(0, rows // BLOCK, build, 0)
+
+    def gather_mats(step, carry):
+        low, high = z - step, z + step
+
+        @pl.when(low >= 0)
+        def _():
+            meta_copy(low, left, meta_left).wait_recv()
+
+            @pl.when(has_right)
+            def _():
+                meta_copy(low, right, meta_right).start()
+
+        @pl.when(high < grids)
+        def _():
+            meta_copy(high, right, meta_right).wait_recv()
+
+            @pl.when(has_left)
+            def _():
+                meta_copy(high, left, meta_left).start()
+
+        @pl.when(low >= 0)
+        def _():
+            build_mats(low)
+
+        @pl.when(high < grids)
+        def _():
+            build_mats(high)
+
+        return carry
+
 
     ahead, behind = [], []
     for d in range(4):
@@ -250,14 +296,17 @@
         before = jnp.where(first, shifted(rows + 1 - stride), shifted(1))
         moved = keep * value + ahead[1] * after + behind[1] * before
         moved = moved + ahead[0] * shifted(rows - stride) + behind[0] * shifted(stride)
-        moved = moved + ahead[3] * pltpu.roll(value, reach - 1, 0)
+        moved = moved + ahead[3] * pltpu.roll(value, value.shape[0] - 1, 0)
         return moved + behind[3] * pltpu.roll(value, 1, 0)
 
-    def surplus_part(chunk):
-        at = pl.ds(chunk * part, reach)
-        value = layers[here, at, :]
-        for table in weights:
-            value = advance(value)
+    def window(chunk):
+        return pl.ds(STARTS[chunk] * unit, SHARES[chunk] * unit + 2 * HALO)
+
+    def surplus_part(chunk, value):
+        at, part = window(chunk), SHARES[chunk] * unit
+        for order, table in enumerate(weights):
+            if order:
+                value = advance(value)
             for offset, factor in table.items():
                 value = value + factor * layers[lax.rem(here + offset, doms), at, :]
         value = jnp.where(inside, value[HALO : HALO + part, :], 0.0)
@@ -265,7 +314,7 @@
         return jnp.where(inside, weight * (both[:part, :] + both[part:, :]), 0.0)
 
     def surplus_copy(slot, chunk, target, send):
-        at = pl.ds(chunk * part, part)
+        at = pl.ds(STARTS[chunk] * unit, SHARES[chunk] * unit)
         return pltpu.make_async_remote_copy(
             src_ref=surplus_of.at[slot, at],
             dst_ref=surplus_of.at[slot, at],
@@ -275,60 +324,76 @@
             device_id_type=MESH,
         )
 
-    right, left = jnp.minimum(z + 1, grids - 1), jnp.maximum(z - 1, 0)
+    def forward(step, chunk):
+        low, high = z - step, z + step
+
+        @pl.when(low >= 0)
+        def _():
+            surplus_copy(low, chunk, left, left_send).wait_recv()
+
+            @pl.when(has_right)
+            def _():
+                surplus_copy(low, chunk, right, right_send).start()
+
+        @pl.when(high < grids)
+        def _():
+            surplus_copy(high, chunk, right, right_send).wait_recv()
+
+            @pl.when(has_left)
+            def _():
+                surplus_copy(high, chunk, left, left_send).start()
 
     for chunk in range(CHUNKS):
-        pass_on(chunk)
+        if chunk == 0:
+            pass_on(0)
+            build_mats(z)
+        value = advance(layers[here, window(chunk), :])
         layer_copy(sibling, chunk, sibling, layer_send.at[0, 0]).wait_recv()
         for slot in sources:
             across = slot + 1 - 2 * core
             layer_copy(across, chunk, sibling, layer_send.at[0, 0]).wait_recv()
-        surplus_of[z, chunk * part : (chunk + 1) * part, :] = surplus_part(chunk)
-
-        @pl.when(z < grids - 1)
+        at = pl.ds(STARTS[chunk] * unit, SHARES[chunk] * unit)
+        surplus_of[z, at, :] = surplus_part(chunk, value)
+
+        @pl.when(has_right)
         def _(chunk=chunk):
             surplus_copy(z, chunk, right, right_send).start()
 
-        @pl.when(z > 0)
+        @pl.when(has_left)
         def _(chunk=chunk):
             surplus_copy(z, chunk, left, left_send).start()
 
-        lax.fori_loop(grids * chunk // CHUNKS, grids * (chunk + 1) // CHUNKS, build_mats, 0)
-
+        if chunk + 1 < CHUNKS:
+            pass_on(chunk + 1)
+        if chunk >= LAG:
+            forward(1, chunk - LAG)
+        begin, end = (max(1, grids * c // CHUNKS) for c in (chunk, chunk + 1))
+        if end > begin:
+            lax.fori_loop(begin, end, gather_mats, 0)
+
+    for chunk in range(CHUNKS - LAG, CHUNKS):
+        forward(1, chunk)
     total[...] = product(mats[z], surplus_of[z])
 
+    def collect(step):
+        low, high = z - step, z + step
+
+        @pl.when(low >= 0)
+        def _():
+            total[...] += product(mats[low], surplus_of[low])
+
+        @pl.when(high < grids)
+        def _():
+            total[...] += product(mats[high], surplus_of[high])
+
     def exchange(step, carry):
-        low, high = z - step, z + step
-
+        collect(step - 1)
         for chunk in range(CHUNKS):
-
-            @pl.when(low >= 0)
-            def _(chunk=chunk):
-                surplus_copy(low, chunk, left, left_send).wait_recv()
-
-                @pl.when(z < grids - 1)
-                def _():
-                    surplus_copy(low, chunk, right, right_send).start()
-
-            @pl.when(high < grids)
-            def _(chunk=chunk):
-                surplus_copy(high, chunk, right, right_send).wait_recv()
-
-                @pl.when(z > 0)
-                def _():
-                    surplus_copy(high, chunk, left, left_send).start()
-
-        @pl.when(low >= 0)
-        def _():
-            total[...] += product(mats[low], surplus_of[low])
-
-        @pl.when(high < grids)
-        def _():
-            total[...] += product(mats[high], surplus_of[high])
-
+            forward(step, chunk)
         return carry
 
-    lax.fori_loop(1, grids, exchange, 0)
+    lax.fori_loop(2, grids, exchange, 0)
+    collect(grids - 1)
 
     own_ref[...] = total[rows : rows + owned, :]
     result_ref[...] = jnp.where(
@@ -340,17 +405,22 @@
             layer_copy(here, piece, peer, layer_send.at[j, piece]).wait_send()
             layer_copy(here, piece, peer, pass_send.at[j, piece]).wait_send()
         layer_copy(here, piece, sibling, layer_send.at[chips - 1, piece]).wait_send()
-    for j in range(grids - 1):
-        meta_copy(j).wait_send()
-
     def drain(slot, carry):
+        @pl.when(has_right & (slot <= z))
+        def _():
+            meta_copy(slot, right, meta_right).wait_send()
+
+        @pl.when(has_left & (slot >= z))
+        def _():
+            meta_copy(slot, left, meta_left).wait_send()
+
         for chunk in range(CHUNKS):
 
-            @pl.when((z < grids - 1) & (slot <= z))
+            @pl.when(has_right & (slot <= z))
             def _(chunk=chunk):
                 surplus_copy(slot, chunk, right, right_send).wait_send()
 
-            @pl.when((z > 0) & (slot >= z))
+            @pl.when(has_left & (slot >= z))
             def _(chunk=chunk):
                 surplus_copy(slot, chunk, left, left_send).wait_send()
 
@@ -365,6 +435,7 @@
     padded = -(-owned // 16) * 16
     chips = doms // 2
     vmem = pl.BlockSpec(memory_space=pltpu.VMEM)
+    hbm = pl.BlockSpec(memory_space=pltpu.HBM)
     smem = pl.BlockSpec(memory_space=pltpu.SMEM)
     sems = pltpu.SemaphoreType.DMA
     own, result = pl.pallas_call(
@@ -373,18 +444,22 @@
             jax.ShapeDtypeStruct((owned, lanes), F32),
             jax.ShapeDtypeStruct((rows, lanes), F32),
         ],
-        in_specs=[smem, smem, smem, vmem, vmem],
+        in_specs=[smem, smem, smem, hbm, hbm],
         out_specs=[vmem, vmem],
         scratch_shapes=[
+            pltpu.VMEM((position.shape[0] // lanes, lanes), jnp.int32),
+            pltpu.VMEM((rows, lanes), F32),
             pltpu.VMEM((doms, lanes + 2 * HALO, rows), F32),
             pltpu.VMEM((grids, 8, rows), F32),
             pltpu.VMEM((rows, rows), BF16),
             pltpu.VMEM((grids, lanes, rows), F32),
             pltpu.VMEM((grids, rows + padded, rows), BF16),
             pltpu.VMEM((rows + padded, lanes), F32),
+            sems((2,)),
             sems((chips, CHUNKS)),
             sems((doms, CHUNKS)),
             sems((chips, CHUNKS)),
+            sems((grids,)),
             sems((grids,)),
             sems((grids,)),
             sems((grids, CHUNKS)),

time: 40.8 us -> 38 us (0.931)
  Pallas kernels: 35.6 us -> 32.8 us
    pallas_call x1, Pallas kernels: 35.6 us -> 32.8 us  [local(): pl.pallas_call(functools.partial(kernel, doms, grids), out_shape=[jax.Sha...]
where the time goes in v2:
time: 38 us; the launch traced here: 37.8 us
  Pallas kernels  32.8 us (86%)
  local copies, waits for them, and re-layouts  3.69 us (10%)
  between operations  1.3 us (3%)
    pallas_call x1, Pallas kernels, local(): pl.pallas_call(functools.partial(kernel, doms, grids), out_shape=[jax.Sha...  32.8 us
    unnamed x10, local copies, waits for them, and re-layouts  3.69 us

profile of v2, /device:TPU:0, one launch (start us, length us, event | category | flops | bytes accessed | tf_op | source)
XLA Modules:
  0.0 37.8 jit_solution(4858266918420264118)
XLA Ops:
  1.3 0.0 copy-start.2
  1.3 0.0 copy-start.3
  1.3 0.6 %copy-done.2 = s32[1,2]{1,0:T(1,128)S(1)} copy-done((s32[1,2]{1,0:T(1,128)S(1)}, s32[1,2]{1,0:T(1,128)}, u32[]{:S(2)}) %copy-start.2) | copy-done | bytes 32
  1.9 0.0 copy-done.3
  1.9 0.0 copy-start
  2.0 0.9 %copy-done = f32[1,512,1,128]{3,2,1,0:T(1,128)S(1)} copy-done((f32[1,512,1,128]{3,2,1,0:T(1,128)S(1)}, f32[1,512,1,128]{3,2,1,0:T(1,128)}, u32[]{:S(2)}) %copy-start) | copy-done | bytes 262168
  2.9 0.0 copy-start.1
  2.9 0.7 %copy-done.1 = s32[1792]{0:T(1024)S(1)} copy-done((s32[1792]{0:T(1024)S(1)}, s32[1792]{0:T(1024)}, u32[]{:S(2)}) %copy-start.1) | copy-done | bytes 7192
  3.6 32.8 %shard_map.68 = (f32[448,128]{1,0:T(8,128)S(1)}, f32[512,128]{1,0:T(8,128)S(1)}) custom-call(s32[1,2]{1,0:T(1,128)S(1)} %copy-done.2, s32[1]{0:T(128)S(6)} %copy.11.coef, f32[4]{0:T(128)S(1)} %copy-done.3, s32[14,128]{1,0:T(8,128)S(1)} %bitcast.11, f32[512,128]{1,0:T(8,128)S(1)} %bitcast.8), custom_call_target="tpu_custom_call" | custom-call | tf_op jit(solution)/shard_map/pallas_call | solution.py:441
  36.4 0.7 %copy.12 = f32[448,1,128]{2,1,0:T(1,128)} copy(f32[448,1,128]{2,1,0:T(1,128)S(1)} %bitcast.10) | data formatting | bytes 458752
  37.1 0.7 %copy.13 = f32[1,512,1,128]{3,2,1,0:T(1,128)} copy(f32[1,512,1,128]{3,2,1,0:T(1,128)S(1)} %bitcast.9) | data formatting | bytes 524288
Async XLA Ops:
  1.3 0.7 %copy-start.2 = (s32[1,2]{1,0:T(1,128)S(1)}, s32[1,2]{1,0:T(1,128)}, u32[]{:S(2)}) copy-start(s32[1,2]{1,0:T(1,128)} %lev.1) | copy-start | bytes 28
  1.3 0.7 %copy-start.3 = (f32[4]{0:T(128)S(1)}, f32[4]{0:T(128)}, u32[]{:S(2)}) copy-start(f32[4]{0:T(128)} %vel.1) | copy-start | bytes 52
  1.9 0.9 %copy-start = (f32[1,512,1,128]{3,2,1,0:T(1,128)S(1)}, f32[1,512,1,128]{3,2,1,0:T(1,128)}, u32[]{:S(2)}) copy-start(f32[1,512,1,128]{3,2,1,0:T(1,128)} %param.5) | copy-start | bytes 786436
  2.9 0.7 %copy-start.1 = (s32[1792]{0:T(1024)S(1)}, s32[1792]{0:T(1024)}, u32[]{:S(2)}) copy-start(s32[1792]{0:T(1024)} %param.9) | copy-start | bytes 21508

commit v3 on v2

--- a/solution.py
+++ b/solution.py
@@ -18,6 +18,7 @@
 CHUNKS = len(SHARES)
 STARTS = [sum(SHARES[:c]) for c in range(CHUNKS + 1)]
 LAG = 2
+AHEAD = 2
 HALO = 8
 BLOCK = 64
 MESH = pl.DeviceIdType.MESH
@@ -152,9 +153,12 @@
 
     neighbours = has_right.astype(jnp.int32) + has_left.astype(jnp.int32)
     pl.semaphore_wait(barrier, chips + neighbours)
-    for piece in range(CHUNKS):
+    def send_across(piece):
         for j, peer in enumerate(others):
             layer_copy(here, piece, peer, layer_send.at[j, piece]).start()
+
+    for piece in range(AHEAD):
+        send_across(piece)
     for piece in range(CHUNKS):
         layer_copy(here, piece, sibling, layer_send.at[chips - 1, piece]).start()
 
@@ -179,6 +183,9 @@
     def pass_on(piece):
         for j, slot in enumerate(sources):
             layer_copy(slot, piece, sibling, layer_send.at[0, 0]).wait_recv()
+        if piece + AHEAD < CHUNKS:
+            send_across(piece + AHEAD)
+        for j, slot in enumerate(sources):
             layer_copy(slot, piece, sibling, pass_send.at[j, piece]).start()
 
     inside = flat < live
@@ -387,8 +394,9 @@
             total[...] += product(mats[high], surplus_of[high])
 
     def exchange(step, carry):
+        forward(step, 0)
         collect(step - 1)
-        for chunk in range(CHUNKS):
+        for chunk in range(1, CHUNKS):
             forward(step, chunk)
         return carry
 

time: 38 us -> 37.9 us (level)
  no operation moved by 1% of the time
where the time goes in v3:
time: 37.9 us; the launch traced here: 37.7 us
  Pallas kernels  32.7 us (86%)
  local copies, waits for them, and re-layouts  3.69 us (10%)
  between operations  1.3 us (3%)
    pallas_call x1, Pallas kernels, local(): pl.pallas_call(functools.partial(kernel, doms, grids), out_shape=[jax.Sha...  32.7 us
    unnamed x10, local copies, waits for them, and re-layouts  3.69 us

profile of v3, /device:TPU:0, one launch (start us, length us, event | category | flops | bytes accessed | tf_op | source)
XLA Modules:
  0.0 37.7 jit_solution(13925644208230505)
XLA Ops:
  1.3 0.0 copy-start.2
  1.3 0.0 copy-start.3
  1.3 0.6 %copy-done.2 = s32[1,2]{1,0:T(1,128)S(1)} copy-done((s32[1,2]{1,0:T(1,128)S(1)}, s32[1,2]{1,0:T(1,128)}, u32[]{:S(2)}) %copy-start.2) | copy-done | bytes 32
  1.9 0.0 copy-done.3
  1.9 0.0 copy-start
  2.0 0.9 %copy-done = f32[1,512,1,128]{3,2,1,0:T(1,128)S(1)} copy-done((f32[1,512,1,128]{3,2,1,0:T(1,128)S(1)}, f32[1,512,1,128]{3,2,1,0:T(1,128)}, u32[]{:S(2)}) %copy-start) | copy-done | bytes 262168
  2.9 0.0 copy-start.1
  2.9 0.7 %copy-done.1 = s32[1792]{0:T(1024)S(1)} copy-done((s32[1792]{0:T(1024)S(1)}, s32[1792]{0:T(1024)}, u32[]{:S(2)}) %copy-start.1) | copy-done | bytes 7192
  3.6 32.7 %shard_map.68 = (f32[448,128]{1,0:T(8,128)S(1)}, f32[512,128]{1,0:T(8,128)S(1)}) custom-call(s32[1,2]{1,0:T(1,128)S(1)} %copy-done.2, s32[1]{0:T(128)S(6)} %copy.11.coef, f32[4]{0:T(128)S(1)} %copy-done.3, s32[14,128]{1,0:T(8,128)S(1)} %bitcast.11, f32[512,128]{1,0:T(8,128)S(1)} %bitcast.8), custom_call_target="tpu_custom_call" | custom-call | tf_op jit(solution)/shard_map/pallas_call | solution.py:449
  36.3 0.7 %copy.12 = f32[448,1,128]{2,1,0:T(1,128)} copy(f32[448,1,128]{2,1,0:T(1,128)S(1)} %bitcast.10) | data formatting | bytes 458752
  37.0 0.7 %copy.13 = f32[1,512,1,128]{3,2,1,0:T(1,128)} copy(f32[1,512,1,128]{3,2,1,0:T(1,128)S(1)} %bitcast.9) | data formatting | bytes 524288
Async XLA Ops:
  1.3 0.7 %copy-start.2 = (s32[1,2]{1,0:T(1,128)S(1)}, s32[1,2]{1,0:T(1,128)}, u32[]{:S(2)}) copy-start(s32[1,2]{1,0:T(1,128)} %lev.1) | copy-start | bytes 28
  1.3 0.7 %copy-start.3 = (f32[4]{0:T(128)S(1)}, f32[4]{0:T(128)}, u32[]{:S(2)}) copy-start(f32[4]{0:T(128)} %vel.1) | copy-start | bytes 52
  1.9 0.9 %copy-start = (f32[1,512,1,128]{3,2,1,0:T(1,128)S(1)}, f32[1,512,1,128]{3,2,1,0:T(1,128)}, u32[]{:S(2)}) copy-start(f32[1,512,1,128]{3,2,1,0:T(1,128)} %param.5) | copy-start | bytes 786436
  2.9 0.7 %copy-start.1 = (s32[1792]{0:T(1024)S(1)}, s32[1792]{0:T(1024)}, u32[]{:S(2)}) copy-start(s32[1792]{0:T(1024)} %param.9) | copy-start | bytes 21508
